TPU v7x, 256 devices: a whole 4x4x8 slice. The times are simulated.
256 devices in a mesh: tm: 16 (over z, y_hi), rows: 16 (over y_lo, x, core).
Axes of the slice: x: 4, y: 4 (y_hi: 2, y_lo: 2; y = y_hi * 2 + y_lo), z: 8, core: 2. Of those that a mesh axis runs over, the one named last changes fastest.
Arguments:
- features: bfloat16 [64, 128, 512, 128], P('tm', 'rows'), may hold values from -6 to 6
- decoder_weight: bfloat16 [3, 3, 3, 128, 128], replicated, may hold values from -0.109375 to 0.109375
- decoder_bias: float32 [128], replicated, may hold values from -3 to 3
- critic_weight: bfloat16 [3, 3, 3, 128, 256], replicated, may hold values from -0.109375 to 0.109375
- critic_bias: float32 [256], replicated, may hold values from -3 to 3
Outputs:
- decoded: bfloat16 [64, 128, 512, 128], P('tm', 'rows')
- critic_features: bfloat16 [32, 64, 256, 256], P('tm', 'rows')
All inputs are finite; a program needn't handle non-finite values.
Results may differ from a plain program's by a relative error of at most 0.0049.
Values may be sent and summed in bfloat16 or wider, within the bound.
A program may use at most 128 MiB of HBM per device.

v0:
```python
import jax
import jax.numpy as jnp
from jax import lax
from jax.experimental import pallas as pl
from jax.experimental.pallas import tpu as pltpu
from jax.sharding import PartitionSpec as P

MESH = pl.DeviceIdType.MESH
BF = jnp.bfloat16
F32 = jnp.float32
ORDER = (7, 0, 6, 5, 4, 3, 2, 1)


def kernel(feat, w, db, cw, cb, out, cout,
           fv, act, wt, cwv, dbv, cbv, dec, cact, dech, part, cacc, qout, qin, co, scr,
           loc, osem, csem, tms, tmr, qs, qr, ups, upr, dns, dnr):
    tm = lax.axis_index("tm")
    row = lax.axis_index("rows")
    n_tm = lax.axis_size("tm")
    n_row = lax.axis_size("rows")
    has_next = tm < n_tm - 1
    has_prev = tm > 0
    has_up = row < n_row - 1
    has_dn = row > 0
    nxt = (lax.rem(tm + 1, n_tm), row)
    prv = (lax.rem(tm + n_tm - 1, n_tm), row)
    up = (tm, lax.rem(row + 1, n_row))
    dn = (tm, lax.rem(row + n_row - 1, n_row))

    local = [
        pltpu.make_async_copy(feat, fv.at[pl.ds(2, 4), pl.ds(1, 8)], loc.at[0]),
        pltpu.make_async_copy(cw, cwv, loc.at[1]),
        pltpu.make_async_copy(w, wt.at[:, pl.ds(0, 1152), pl.ds(0, 128)], loc.at[2]),
        pltpu.make_async_copy(w, wt.at[:, pl.ds(384, 1152), pl.ds(128, 128)], loc.at[3]),
        pltpu.make_async_copy(db, dbv, loc.at[4]),
        pltpu.make_async_copy(cb, cbv, loc.at[5]),
    ]
    for c in local:
        c.start()

    barrier = pltpu.get_barrier_semaphore()
    count = 0
    for ok, dev in ((has_next, nxt), (has_prev, prv), (has_up, up), (has_dn, dn)):
        @pl.when(ok)
        def _():
            pl.semaphore_signal(barrier, inc=1, device_id=dev, device_id_type=MESH)
        count = count + ok.astype(jnp.int32)
    pl.semaphore_wait(barrier, count)

    def remote(src, dst, ss, rs, dev):
        return pltpu.make_async_remote_copy(
            src_ref=src, dst_ref=dst, send_sem=ss, recv_sem=rs, device_id=dev, device_id_type=MESH)

    feats = [remote(feat.at[pl.ds(2, 2), h], fv.at[pl.ds(0, 2), h + 1], tms.at[k], tmr.at[k], nxt)
             for k, h in enumerate(ORDER)]
    own_up = remote(feat.at[:, 7], fv.at[pl.ds(2, 4), 0], ups.at[0], upr.at[0], up)
    own_dn = remote(feat.at[:, 0], fv.at[pl.ds(2, 4), 9], dns.at[0], dnr.at[0], dn)
    fwd_up = remote(fv.at[pl.ds(0, 2), 8], fv.at[pl.ds(0, 2), 0], ups.at[1], upr.at[1], up)
    fwd_dn = remote(fv.at[pl.ds(0, 2), 1], fv.at[pl.ds(0, 2), 9], dns.at[1], dnr.at[1], dn)
    decs = [remote(dec.at[f, 7], dech.at[f], ups.at[2 + f], upr.at[2 + f], up) for f in range(4)]
    quot = [remote(qout.at[j], qin.at[j], qs.at[j], qr.at[j], nxt) for j in range(4)]

    @pl.when(has_up)
    def _():
        own_up.start()

    @pl.when(has_dn)
    def _():
        own_dn.start()

    @pl.when(has_next)
    def _():
        for c in feats:
            c.start()

    zrow = jnp.zeros((512, 128), BF)

    @pl.when(jnp.logical_not(has_dn))
    def _():
        @pl.loop(0, 6)
        def _(f):
            fv[f, 0] = zrow

        @pl.loop(0, 4)
        def _(f):
            dech[f] = zrow

    @pl.when(jnp.logical_not(has_up))
    def _():
        @pl.loop(0, 6)
        def _(f):
            fv[f, 9] = zrow

    @pl.when(jnp.logical_not(has_prev))
    def _():
        @pl.loop(0, 2)
        def _(f):
            @pl.loop(0, 10)
            def _(h):
                fv[f, h] = zrow

        @pl.loop(0, 4)
        def _(j):
            qin[j] = jnp.zeros((256, 256), BF)

    for s in range(2):
        scr[s, 0:8] = jnp.zeros((8, 128), F32)
        scr[s, 520:528] = jnp.zeros((8, 128), F32)
    for t in range(3):
        wt[t, 1152:1536, 0:128] = jnp.zeros((384, 128), BF)
        wt[t, 0:384, 128:256] = jnp.zeros((384, 128), BF)

    for c in local:
        c.wait()

    def prep(f, h):
        half = 0.5 * fv[f, h].astype(F32)
        a = half + half * jnp.tanh(half)
        scr[0, 8:520] = a
        base = pl.multiple_of(h * 384, 128)
        act[f, :, pl.ds(base, 128)] = scr[0, 7:519].astype(BF)
        act[f, :, pl.ds(base + 128, 128)] = a.astype(BF)
        act[f, :, pl.ds(base + 256, 128)] = scr[0, 9:521].astype(BF)

    def cprep(f, h, d):
        scr[1, 8:520] = d.astype(F32)
        base = pl.multiple_of(h * 384, 128)
        cact[f, :, pl.ds(base, 128)] = scr[1, pl.ds(7, 256, stride=2)].astype(BF)
        cact[f, :, pl.ds(base + 128, 128)] = scr[1, pl.ds(8, 256, stride=2)].astype(BF)
        cact[f, :, pl.ds(base + 256, 128)] = scr[1, pl.ds(9, 256, stride=2)].astype(BF)

    def taps(first, p, which):
        lanes = pl.ds(pl.multiple_of(p * 768, 128), 1536)
        total = None
        for t in which:
            d = jnp.dot(act[first + t, :, lanes], wt[t], preferred_element_type=F32)
            total = d if total is None else total + d
        return total

    def out_copy(f, p):
        rows2 = pl.ds(p * 2, 2)
        return pltpu.make_async_copy(dec.at[f, rows2], out.at[f, rows2], osem.at[f, p])

    def finish(f, p, total):
        for o in range(2):
            h = 2 * p + o
            y = total[:, o * 128:(o + 1) * 128] + fv[f + 2, h + 1].astype(F32) + dbv[...]
            d = y.astype(BF)
            dec[f, h] = d
            cprep(f, h + 1, d)
        out_copy(f, p).start()

    def critic(f, t, j):
        lanes = pl.ds(pl.multiple_of(j * 768, 128), 1152)
        return jnp.dot(cact[f, :, lanes], cwv[t], preferred_element_type=F32)

    @pl.loop(3, 6)
    def _(f):
        @pl.loop(1, 9)
        def _(h):
            prep(f, h)

    @pl.when(has_up)
    def _():
        own_up.wait_send()
        own_dn_recv = remote(feat.at[:, 0], fv.at[pl.ds(2, 4), 9], dns.at[0], dnr.at[0], dn)
        own_dn_recv.wait_recv()

    @pl.when(has_dn)
    def _():
        own_dn.wait_send()
        own_up.wait_recv()

    @pl.loop(3, 6)
    def _(f):
        prep(f, 0)
        prep(f, 9)

    def decode(f):
        @pl.loop(0, 4)
        def _(i):
            p = 3 - i
            finish(f, p, taps(f, p, (0, 1, 2)))

        @pl.when(has_up)
        def _():
            decs[f].start()

    decode(3)

    @pl.when(has_prev)
    def _():
        feats[0].wait_recv()
        feats[1].wait_recv()

        @pl.when(has_up)
        def _():
            fwd_up.start()

        @pl.when(has_dn)
        def _():
            fwd_dn.start()

    @pl.loop(0, 10)
    def _(h):
        prep(2, h)

    decode(2)

    def halo_dec(f):
        @pl.when(has_dn)
        def _():
            decs[f].wait_recv()
        cprep(f, 0, dech[f])

    halo_dec(3)

    @pl.loop(0, 4)
    def _(j):
        qout[j] = critic(3, 0, j).astype(BF)

    @pl.when(has_next)
    def _():
        for c in quot:
            c.start()

    halo_dec(2)

    @pl.loop(0, 4)
    def _(j):
        cacc[1, j] = critic(2, 1, j) + critic(3, 2, j)

    @pl.loop(0, 4)
    def _(p):
        part[0, p] = taps(0, p, (2,))
        part[1, p] = taps(1, p, (1, 2))

    def arrived(k):
        @pl.when(has_prev)
        def _():
            feats[k].wait_recv()

    def prep2(h):
        prep(0, h)
        prep(1, h)

    prep2(8)
    prep2(1)

    @pl.when(jnp.logical_and(has_prev, has_up))
    def _():
        fwd_dn.wait_recv()

    prep2(9)

    @pl.when(jnp.logical_and(has_prev, has_dn))
    def _():
        fwd_up.wait_recv()

    prep2(0)

    def rest(p):
        finish(0, p, part[0, p] + taps(0, p, (0, 1)))
        finish(1, p, part[1, p] + taps(1, p, (0,)))

    for k, pairs in ((2, ()), (3, (3,)), (4, ()), (5, (2,)), (6, ()), (7, (1, 0))):
        arrived(k)
        prep2(ORDER[k] + 1)
        for p in pairs:
            rest(p)
            if p == 3:
                @pl.when(has_up)
                def _():
                    decs[0].start()
                    decs[1].start()

    halo_dec(0)
    halo_dec(1)

    def c_copy(c, j):
        return pltpu.make_async_copy(co.at[c, j], cout.at[c, j], csem.at[c, j])

    def leaky(v):
        return jnp.where(v > 0, v, 0.2 * v).astype(BF)

    @pl.loop(0, 4)
    def _(j):
        cacc[0, j] = critic(0, 1, j) + critic(1, 2, j)
        co[1, j] = leaky(cacc[1, j] + critic(1, 0, j) + cbv[...])
        c_copy(1, j).start()

    for j in range(4):
        @pl.when(has_prev)
        def _():
            quot[j].wait_recv()
        co[0, j] = leaky(cacc[0, j] + qin[j].astype(F32) + cbv[...])
        c_copy(0, j).start()

    @pl.when(has_next)
    def _():
        for c in feats:
            c.wait_send()
        for c in quot:
            c.wait_send()

    @pl.when(has_up)
    def _():
        for c in decs:
            c.wait_send()

    @pl.when(jnp.logical_and(has_prev, has_up))
    def _():
        fwd_up.wait_send()

    @pl.when(jnp.logical_and(has_prev, has_dn))
    def _():
        fwd_dn.wait_send()

    for f in range(4):
        for p in range(4):
            out_copy(f, p).wait()
    for c in range(2):
        for j in range(4):
            c_copy(c, j).wait()


def shards(features, decoder_weight, decoder_bias, critic_weight, critic_bias):
    V = pltpu.VMEM
    dma = pltpu.SemaphoreType.DMA
    anyspace = pl.BlockSpec(memory_space=pl.ANY)
    return pl.pallas_call(
        kernel,
        out_shape=(jax.ShapeDtypeStruct((4, 8, 512, 128), BF), jax.ShapeDtypeStruct((2, 4, 256, 256), BF)),
        in_specs=[anyspace] * 5,
        out_specs=(anyspace, anyspace),
        scratch_shapes=[
            V((6, 10, 512, 128), BF),
            V((6, 512, 3840), BF),
            V((3, 1536, 256), BF),
            V((3, 1152, 256), BF),
            V((1, 128), F32),
            V((1, 256), F32),
            V((4, 8, 512, 128), BF),
            V((4, 256, 3456), BF),
            V((4, 512, 128), BF),
            V((2, 4, 512, 256), F32),
            V((2, 4, 256, 256), F32),
            V((4, 256, 256), BF),
            V((4, 256, 256), BF),
            V((2, 4, 256, 256), BF),
            V((2, 528, 128), F32),
            dma((6,)), dma((4, 4)), dma((2, 4)),
            dma((8,)), dma((8,)), dma((4,)), dma((4,)),
            dma((6,)), dma((6,)), dma((2,)), dma((2,)),
        ],
        compiler_params=pltpu.CompilerParams(
            collective_id=0, has_side_effects=True, vmem_limit_bytes=62 << 20),
        cost_estimate=pl.CostEstimate(flops=40_000_000_000, bytes_accessed=20_000_000, transcendentals=4_000_000),
        name="tokenizer",
    )(
        features,
        decoder_weight.reshape(3, 1152, 128),
        decoder_bias.reshape(1, 128),
        critic_weight.reshape(3, 1152, 256),
        critic_bias.reshape(1, 256),
    )


def solution(mesh):
    in_specs = (P("tm", "rows", None, None), P(), P(), P(), P())
    out_specs = (P("tm", "rows", None, None), P("tm", "rows", None, None))
    return jax.shard_map(shards, mesh=mesh, in_specs=in_specs, out_specs=out_specs, check_vma=False)
```

profile of v0, /device:TPU:129, one launch (start us, length us, event | category | flops | bytes accessed | tf_op | source)
XLA Modules:
  0.0 83.4 jit_solution(7784045623837497075)
XLA Ops:
  0.6 77.0 %tokenizer.1 = (bf16[4,8,512,128]{3,2,1,0:T(8,128)(2,1)}, bf16[2,4,256,256]{3,2,1,0:T(8,128)(2,1)}) custom-call(bf16[4,8,512,128]{3,2,1,0:T(8,128)(2,1)} %feat.1, bf16[3,1152,128]{2,1,0:T(8,128)(2,1)} %bitcast.5, f32[1,128]{1,0:T(1,128)} %bitcast.7, bf16[3,1152,256]{2,1,0:T(8,128)(2,1)} %bitcast.4, f32[1,256]{1,0:T(1,128)} %bitcast.6), custom_call_target="tpu_custom_call" | custom-call | flops 40000000000 | bytes 20000000 | tf_op jit(solution)/shard_map/tokenizer/pallas_call | solution.py:331
  77.6 0.0 copy-start
  77.6 4.7 %copy.9 = bf16[4,8,512,128]{3,2,1,0:T(8,128)(2,1)} copy(bf16[4,8,512,128]{3,2,1,0:T(8,128)(2,1)} %get-tuple-element.4) | data formatting | bytes 8388608
  82.4 0.0 copy-done
  82.4 1.0 %copy.10 = bf16[2,4,256,256]{3,2,1,0:T(8,128)(2,1)} copy(bf16[2,4,256,256]{3,2,1,0:T(8,128)(2,1)S(1)} %copy-done) | data formatting | bytes 2097152
Async XLA Ops:
  77.6 4.8 %copy-start = (bf16[2,4,256,256]{3,2,1,0:T(8,128)(2,1)S(1)}, bf16[2,4,256,256]{3,2,1,0:T(8,128)(2,1)}, u32[]{:S(2)}) copy-start(bf16[2,4,256,256]{3,2,1,0:T(8,128)(2,1)} %get-tuple-element.5) | copy-start | bytes 3145732
where the time goes:
time: 84.3 us; the launch traced here: 83.4 us
  Pallas kernels  77 us (91%)
  local copies, waits for them, and re-layouts  5.72 us (7%)
    pallas_call x1, Pallas kernels, shards(): pl.pallas_call(kernel, out_shape=(jax.ShapeDtypeStruct((4, 8, 512, 128),...  77 us
    unnamed x4, local copies, waits for them, and re-layouts  5.72 us

commit v1 on v0

--- a/solution.py
+++ b/solution.py
@@ -11,9 +11,9 @@
 ORDER = (7, 0, 6, 5, 4, 3, 2, 1)
 
 
-def kernel(feat, w, db, cw, cb, out, cout,
-           fv, act, wt, cwv, dbv, cbv, dec, cact, dech, part, cacc, qout, qin, co, scr,
-           loc, osem, csem, tms, tmr, qs, qr, ups, upr, dns, dnr):
+def kernel(feat, w, db, cw, cb, dec, co,
+           fv, act, wt, cwv, dbv, cbv, cact, dech, part, cacc, qout, qin, scr,
+           rbuf, rbs, rbr, loc, tms, tmr, qs, qr, ups, upr, dns, dnr):
     tm = lax.axis_index("tm")
     row = lax.axis_index("rows")
     n_tm = lax.axis_size("tm")
@@ -38,9 +38,21 @@
     for c in local:
         c.start()
 
+    mid = n_row // 2
+    shed = ((0, 2, (3, 4)), (1, 6, (3,)), (n_row - 2, n_row - 3, (3,)), (n_row - 1, mid + 1, (3,)))
+
     barrier = pltpu.get_barrier_semaphore()
     count = 0
-    for ok, dev in ((has_next, nxt), (has_prev, prv), (has_up, up), (has_dn, dn)):
+    pairs = [(has_next, nxt), (has_prev, prv), (has_up, up), (has_dn, dn)]
+    for r, via, _ in shed:
+        at_r, at_via = row == r, row == via
+        pairs += [
+            (jnp.logical_and(has_next, at_r), (nxt[0], via)),
+            (jnp.logical_and(has_prev, at_r), (tm, via)),
+            (jnp.logical_and(has_prev, at_via), (prv[0], r)),
+            (jnp.logical_and(has_prev, at_via), (tm, r)),
+        ]
+    for ok, dev in pairs:
         @pl.when(ok)
         def _():
             pl.semaphore_signal(barrier, inc=1, device_id=dev, device_id_type=MESH)
@@ -68,10 +80,27 @@
     def _():
         own_dn.start()
 
-    @pl.when(has_next)
-    def _():
-        for c in feats:
-            c.start()
+    def detour(r, via, places, k):
+        slot = places.index(k)
+        return remote(feat.at[pl.ds(2, 2), ORDER[k]], rbuf.at[slot], tms.at[k], rbr.at[slot], (nxt[0], via))
+
+    def onward(r, via, places, k):
+        slot = places.index(k)
+        return remote(rbuf.at[slot], fv.at[pl.ds(0, 2), ORDER[k] + 1], rbs.at[slot], tmr.at[k], (tm, r))
+
+    for k in range(8):
+        direct = has_next
+        for r, via, places in shed:
+            if k in places:
+                direct = jnp.logical_and(direct, row != r)
+
+                @pl.when(jnp.logical_and(has_next, row == r))
+                def _():
+                    detour(r, via, places, k).start()
+
+        @pl.when(direct)
+        def _():
+            feats[k].start()
 
     zrow = jnp.zeros((512, 128), BF)
 
@@ -137,10 +166,6 @@
             total = d if total is None else total + d
         return total
 
-    def out_copy(f, p):
-        rows2 = pl.ds(p * 2, 2)
-        return pltpu.make_async_copy(dec.at[f, rows2], out.at[f, rows2], osem.at[f, p])
-
     def finish(f, p, total):
         for o in range(2):
             h = 2 * p + o
@@ -148,7 +173,6 @@
             d = y.astype(BF)
             dec[f, h] = d
             cprep(f, h + 1, d)
-        out_copy(f, p).start()
 
     def critic(f, t, j):
         lanes = pl.ds(pl.multiple_of(j * 768, 128), 1152)
@@ -229,6 +253,13 @@
     @pl.loop(0, 4)
     def _(j):
         cacc[1, j] = critic(2, 1, j) + critic(3, 2, j)
+
+    for r, via, places in shed:
+        @pl.when(jnp.logical_and(has_prev, row == via))
+        def _():
+            for k in places:
+                detour(r, via, places, k).wait_recv()
+                onward(r, via, places, k).start()
 
     @pl.loop(0, 4)
     def _(p):
@@ -277,9 +308,6 @@
     halo_dec(0)
     halo_dec(1)
 
-    def c_copy(c, j):
-        return pltpu.make_async_copy(co.at[c, j], cout.at[c, j], csem.at[c, j])
-
     def leaky(v):
         return jnp.where(v > 0, v, 0.2 * v).astype(BF)
 
@@ -287,14 +315,18 @@
     def _(j):
         cacc[0, j] = critic(0, 1, j) + critic(1, 2, j)
         co[1, j] = leaky(cacc[1, j] + critic(1, 0, j) + cbv[...])
-        c_copy(1, j).start()
 
     for j in range(4):
         @pl.when(has_prev)
         def _():
             quot[j].wait_recv()
         co[0, j] = leaky(cacc[0, j] + qin[j].astype(F32) + cbv[...])
-        c_copy(0, j).start()
+
+    for r, via, places in shed:
+        @pl.when(jnp.logical_and(has_prev, row == via))
+        def _():
+            for k in places:
+                onward(r, via, places, k).wait_send()
 
     @pl.when(has_next)
     def _():
@@ -316,23 +348,25 @@
     def _():
         fwd_dn.wait_send()
 
-    for f in range(4):
-        for p in range(4):
-            out_copy(f, p).wait()
-    for c in range(2):
-        for j in range(4):
-            c_copy(c, j).wait()
+
+def store(dec, co, out, cout, sems):
+    copies = [pltpu.make_async_copy(dec.at[f], out.at[f], sems.at[f]) for f in range(4)]
+    copies += [pltpu.make_async_copy(co.at[c], cout.at[c], sems.at[4 + c]) for c in range(2)]
+    for c in copies:
+        c.start()
+    for c in copies:
+        c.wait()
 
 
 def shards(features, decoder_weight, decoder_bias, critic_weight, critic_bias):
     V = pltpu.VMEM
     dma = pltpu.SemaphoreType.DMA
     anyspace = pl.BlockSpec(memory_space=pl.ANY)
-    return pl.pallas_call(
+    results = pl.pallas_call(
         kernel,
-        out_shape=(jax.ShapeDtypeStruct((4, 8, 512, 128), BF), jax.ShapeDtypeStruct((2, 4, 256, 256), BF)),
+        out_shape=(pltpu.VMEM((4, 8, 512, 128), BF), pltpu.VMEM((2, 4, 256, 256), BF)),
         in_specs=[anyspace] * 5,
-        out_specs=(anyspace, anyspace),
+        out_specs=(pl.BlockSpec(memory_space=pltpu.VMEM),) * 2,
         scratch_shapes=[
             V((6, 10, 512, 128), BF),
             V((6, 512, 3840), BF),
@@ -340,21 +374,20 @@
             V((3, 1152, 256), BF),
             V((1, 128), F32),
             V((1, 256), F32),
-            V((4, 8, 512, 128), BF),
             V((4, 256, 3456), BF),
             V((4, 512, 128), BF),
             V((2, 4, 512, 256), F32),
             V((2, 4, 256, 256), F32),
             V((4, 256, 256), BF),
             V((4, 256, 256), BF),
-            V((2, 4, 256, 256), BF),
             V((2, 528, 128), F32),
-            dma((6,)), dma((4, 4)), dma((2, 4)),
+            V((2, 2, 512, 128), BF),
+            dma((2,)), dma((2,)), dma((6,)),
             dma((8,)), dma((8,)), dma((4,)), dma((4,)),
             dma((6,)), dma((6,)), dma((2,)), dma((2,)),
         ],
         compiler_params=pltpu.CompilerParams(
-            collective_id=0, has_side_effects=True, vmem_limit_bytes=62 << 20),
+            collective_id=0, has_side_effects=True, vmem_limit_bytes=54 << 20),
         cost_estimate=pl.CostEstimate(flops=40_000_000_000, bytes_accessed=20_000_000, transcendentals=4_000_000),
         name="tokenizer",
     )(
@@ -364,6 +397,15 @@
         critic_weight.reshape(3, 1152, 256),
         critic_bias.reshape(1, 256),
     )
+    return pl.pallas_call(
+        store,
+        out_shape=(jax.ShapeDtypeStruct((4, 8, 512, 128), BF), jax.ShapeDtypeStruct((2, 4, 256, 256), BF)),
+        in_specs=[anyspace] * 2,
+        out_specs=(anyspace, anyspace),
+        scratch_shapes=[dma((6,))],
+        compiler_params=pltpu.CompilerParams(vmem_limit_bytes=1 << 20),
+        name="store",
+    )(*results)
 
 
 def solution(mesh):

time: 84.3 us -> 76 us (0.902); the launches traced: 83.4 us -> 75.9 us
  local copies, waits for them, and re-layouts: 5.72 us -> 0 us
  Pallas kernels: 77 us -> 75.3 us
    unnamed x4 -> x0, local copies, waits for them, and re-layouts: 5.72 us -> none
    pallas_call x1 -> x2, Pallas kernels: 77 us -> 75.3 us  [the longest x1 72.9 us: shards(): pl.pallas_call(kernel, out_shape=(pltpu.VMEM((4, 8, 512, 128), BF), pltpu...]
where the time goes in v1:
time: 76 us; the launch traced here: 75.9 us
  Pallas kernels  75.3 us (99%)
    pallas_call x1, Pallas kernels, shards(): pl.pallas_call(kernel, out_shape=(pltpu.VMEM((4, 8, 512, 128), BF), pltpu...  72.9 us
    pallas_call x1, Pallas kernels, shards(): pl.pallas_call(store, out_shape=(jax.ShapeDtypeStruct((4, 8, 512, 128), B...  2.39 us

profile of v1, /device:TPU:129, one launch (start us, length us, event | category | flops | bytes accessed | tf_op | source)
XLA Modules:
  0.0 75.9 jit_solution(661223841523441312)
XLA Ops:
  0.6 72.9 %tokenizer.1 = (bf16[4,8,512,128]{3,2,1,0:T(8,128)(2,1)S(1)}, bf16[2,4,256,256]{3,2,1,0:T(8,128)(2,1)S(1)}) custom-call(bf16[4,8,512,128]{3,2,1,0:T(8,128)(2,1)} %feat.1, bf16[3,1152,128]{2,1,0:T(8,128)(2,1)} %bitcast.5, f32[1,128]{1,0:T(1,128)} %bitcast.7, bf16[3,1152,256]{2,1,0:T(8,128)(2,1)} %bitcast.4, f32[1,256]{1,0:T(1,128)} %bitcast.6), custom_call_target="tpu_custom_call" | custom-call | flops 40000000000 | bytes 20000000 | tf_op jit(solution)/shard_map/tokenizer/pallas_call | solution.py:365
  73.5 2.4 %store.1 = (bf16[4,8,512,128]{3,2,1,0:T(8,128)(2,1)}, bf16[2,4,256,256]{3,2,1,0:T(8,128)(2,1)}) custom-call(bf16[4,8,512,128]{3,2,1,0:T(8,128)(2,1)S(1)} %get-tuple-element.4.dec, bf16[2,4,256,256]{3,2,1,0:T(8,128)(2,1)S(1)} %get-tuple-element.5.co), custom_call_target="tpu_custom_call" | custom-call | tf_op jit(solution)/shard_map/store/pallas_call | solution.py:400

commit v2 on v1

--- a/solution.py
+++ b/solution.py
@@ -294,27 +294,30 @@
         finish(0, p, part[0, p] + taps(0, p, (0, 1)))
         finish(1, p, part[1, p] + taps(1, p, (0,)))
 
+    def leaky(v):
+        return jnp.where(v > 0, v, 0.2 * v).astype(BF)
+
+    def local_critic(j):
+        cacc[0, j] = critic(0, 1, j) + critic(1, 2, j)
+        co[1, j] = leaky(cacc[1, j] + critic(1, 0, j) + cbv[...])
+
     for k, pairs in ((2, ()), (3, (3,)), (4, ()), (5, (2,)), (6, ()), (7, (1, 0))):
         arrived(k)
         prep2(ORDER[k] + 1)
         for p in pairs:
             rest(p)
+            if p < 3:
+                local_critic(p + 1)
             if p == 3:
                 @pl.when(has_up)
                 def _():
                     decs[0].start()
                     decs[1].start()
 
+
     halo_dec(0)
     halo_dec(1)
-
-    def leaky(v):
-        return jnp.where(v > 0, v, 0.2 * v).astype(BF)
-
-    @pl.loop(0, 4)
-    def _(j):
-        cacc[0, j] = critic(0, 1, j) + critic(1, 2, j)
-        co[1, j] = leaky(cacc[1, j] + critic(1, 0, j) + cbv[...])
+    local_critic(0)
 
     for j in range(4):
         @pl.when(has_prev)

time: 76 us -> 76 us (level)
  no operation moved by 1% of the time
where the time goes in v2:
time: 76 us; the launch traced here: 75.9 us
  Pallas kernels  75.3 us (99%)
    pallas_call x1, Pallas kernels, shards(): pl.pallas_call(kernel, out_shape=(pltpu.VMEM((4, 8, 512, 128), BF), pltpu...  72.9 us
    pallas_call x1, Pallas kernels, shards(): pl.pallas_call(store, out_shape=(jax.ShapeDtypeStruct((4, 8, 512, 128), B...  2.39 us

profile of v2, /device:TPU:129, one launch (start us, length us, event | category | flops | bytes accessed | tf_op | source)
XLA Modules:
  0.0 75.9 jit_solution(6997846762006506328)
XLA Ops:
  0.6 72.9 %tokenizer.1 = (bf16[4,8,512,128]{3,2,1,0:T(8,128)(2,1)S(1)}, bf16[2,4,256,256]{3,2,1,0:T(8,128)(2,1)S(1)}) custom-call(bf16[4,8,512,128]{3,2,1,0:T(8,128)(2,1)} %feat.1, bf16[3,1152,128]{2,1,0:T(8,128)(2,1)} %bitcast.5, f32[1,128]{1,0:T(1,128)} %bitcast.7, bf16[3,1152,256]{2,1,0:T(8,128)(2,1)} %bitcast.4, f32[1,256]{1,0:T(1,128)} %bitcast.6), custom_call_target="tpu_custom_call" | custom-call | flops 40000000000 | bytes 20000000 | tf_op jit(solution)/shard_map/tokenizer/pallas_call | solution.py:368
  73.5 2.4 %store.1 = (bf16[4,8,512,128]{3,2,1,0:T(8,128)(2,1)}, bf16[2,4,256,256]{3,2,1,0:T(8,128)(2,1)}) custom-call(bf16[4,8,512,128]{3,2,1,0:T(8,128)(2,1)S(1)} %get-tuple-element.4.dec, bf16[2,4,256,256]{3,2,1,0:T(8,128)(2,1)S(1)} %get-tuple-element.5.co), custom_call_target="tpu_custom_call" | custom-call | tf_op jit(solution)/shard_map/store/pallas_call | solution.py:403
